TPU v7x, 32 devices: a whole 2x2x4 slice. The times are simulated.
32 devices in a mesh: surf: 8 (over z, x), normal: 4 (over y, core).
Axes of the slice: x: 2, y: 2, z: 4, core: 2. Of those that a mesh axis runs over, the one named last changes fastest.
Arguments:
- profile: bfloat16 [16, 16, 131072], P('normal', None, 'surf'), may hold values from -6 to 6
- wall_weight: bfloat16 [10, 16, 16], P(None, 'normal'), may hold values from -0.375 to 0.375
- block_dest: int32 [1024], replicated, may hold values from 0 to 7, as said below
- col_face: int32 [32768], P(('surf', 'normal')), may hold values from 0 to 16383
- char_state: float32 [8, 128, 32768], P(None, None, ('surf', 'normal')), may hold values from -6 to 6
- char_inverse: bfloat16 [128, 128], replicated, as said below
- react: float32 [8, 8], replicated, may hold values from -2 to 2
- bound_weight: float32 [8, 10], replicated, may hold values from -2 to 2
Outputs:
- char_next: float32 [8, 128, 32768], P(None, None, ('surf', 'normal'))
Inputs may be any that keep to these rules, and one draw needn't show every extreme that they name: `block_dest`: each block of surface patch s (blocks s * 128 to (s + 1) * 128 - 1) names an owner; no owner is named by more than 32 blocks of one patch, every patch names some owner exactly 32 times, and every owner is named by exactly 128 blocks in all. `char_inverse`: inverse of a diagonally dominant conduction matrix; its norm is below one.
All inputs are finite; a program needn't handle non-finite values.
Results may differ from a plain program's by a relative error of at most 0.0047.
Values sent between devices are 32-bit elements; how exact they have to be, the bound alone decides.
A program may use at most 128 MiB of HBM per device.

v0:
```python
import functools

import jax
import jax.numpy as jnp
from jax import lax
from jax.experimental import pallas as pl
from jax.experimental.pallas import tpu as pltpu
from jax.sharding import PartitionSpec as P

STEPS = 8
PIECES = 4
LANES = 128
F32 = jnp.float32
BF = jnp.bfloat16
MESH = pl.DeviceIdType.MESH


def source_kernel(
    nsurf, chips, outc,
    x_ref, w_ref, dest_ref, cf_ref, bw_ref,
    src_ref,
    send_a, own_a, recv_a, chip_b, recv_b, wall_ref, s_ref, cat_ref, key_ref, cf_all, gbuf, rbuf,
    sa_send, sa_recv, sb_send, sb_recv, ss_send, ss_recv, sc_send, sc_recv, sg_send, sg_recv,
):
    surf = lax.axis_index("surf")
    normal = lax.axis_index("normal")
    y, core = normal // 2, normal % 2
    peer = (surf, y * 2 + 1 - core)
    extra = outc - 8
    subs = 8 // extra
    faces = x_ref.shape[2]
    half = faces // 2
    piece = half // PIECES
    sub = piece // subs
    depth = x_ref.shape[0] * x_ref.shape[1]
    nblk = faces // LANES
    groups = piece // LANES

    def chip_peer(k):
        return (surf, lax.rem(y + k, chips) * 2 + core)

    def surf_peer(k):
        return (lax.rem(surf + k, nsurf), normal)

    barrier = pltpu.get_barrier_semaphore()
    pl.semaphore_signal(barrier, inc=1, device_id=peer, device_id_type=MESH)
    for k in range(1, chips):
        pl.semaphore_signal(barrier, inc=1, device_id=chip_peer(k), device_id_type=MESH)

    def greet(k, carry):
        pl.semaphore_signal(barrier, inc=1, device_id=surf_peer(k), device_id_type=MESH)
        return carry

    lax.fori_loop(1, nsurf, greet, 0)

    wide = w_ref[...].astype(F32)
    row = lax.broadcasted_iota(jnp.int32, wide.shape, 0)

    def weights(q):
        keep = jnp.logical_or(row < 8, (row - 8) // extra == q)
        return jnp.where(keep, wide, 0.0).astype(BF)

    placed = [weights(q) for q in range(subs)]

    def partial(which, p):
        rest = None
        main = []
        for q in range(subs):
            start = pl.multiple_of(which * half + p * piece + q * sub, sub)
            x = x_ref[:, :, pl.ds(start, sub)].reshape(depth, sub)
            r = jnp.dot(placed[q], x, preferred_element_type=F32)
            main.append(r[:8])
            rest = r[8:] if rest is None else rest + r[8:]
        return jnp.concatenate(main + [rest], axis=1)

    def copy_a(p):
        return pltpu.make_async_remote_copy(
            src_ref=send_a.at[p], dst_ref=recv_a.at[p], send_sem=sa_send.at[p], recv_sem=sa_recv.at[p],
            device_id=peer, device_id_type=MESH)

    def copy_b(k, p):
        return pltpu.make_async_remote_copy(
            src_ref=chip_b.at[p], dst_ref=recv_b.at[k - 1, p], send_sem=sb_send.at[k - 1, p],
            recv_sem=sb_recv.at[k - 1, p], device_id=chip_peer(k), device_id_type=MESH)

    def copy_s(p):
        start = pl.multiple_of((core * PIECES + p) * groups * 8, groups * 8)
        rows = s_ref.at[pl.ds(start, groups * 8)]
        return pltpu.make_async_remote_copy(
            src_ref=rows, dst_ref=rows, send_sem=ss_send.at[p], recv_sem=ss_recv.at[p],
            device_id=peer, device_id_type=MESH)

    def wait_s(p):
        start = pl.multiple_of(((1 - core) * PIECES + p) * groups * 8, groups * 8)
        rows = s_ref.at[pl.ds(start, groups * 8)]
        return pltpu.make_async_remote_copy(
            src_ref=rows, dst_ref=rows, send_sem=ss_send.at[p], recv_sem=ss_recv.at[p],
            device_id=peer, device_id_type=MESH)

    def copy_c(k):
        return pltpu.make_async_remote_copy(
            src_ref=cf_ref, dst_ref=cf_all.at[k], send_sem=sc_send.at[k], recv_sem=sc_recv.at[k],
            device_id=surf_peer(k), device_id_type=MESH)

    def copy_g(k):
        return pltpu.make_async_remote_copy(
            src_ref=gbuf.at[k], dst_ref=rbuf.at[k], send_sem=sg_send.at[k], recv_sem=sg_recv.at[k],
            device_id=surf_peer(k), device_id_type=MESH)

    send_a[0] = partial(1 - core, 0)
    pl.semaphore_wait(barrier, 1 + chips - 1 + nsurf - 1)
    copy_a(0).start()
    own_a[0] = partial(core, 0)
    for p in range(1, PIECES):
        send_a[p] = partial(1 - core, p)
        copy_a(p).start()
        own_a[p] = partial(core, p)
    for p in range(PIECES):
        copy_a(p).wait_recv()
        chip_b[p] = own_a[p] + recv_a[p]
        for k in range(1, chips):
            copy_b(k, p).start()

    def start_c(k, carry):
        copy_c(k).start()
        return carry

    lax.fori_loop(1, nsurf, start_c, 0)
    cf_all[0] = cf_ref[...]

    line = lax.broadcasted_iota(jnp.int32, (nblk, nblk), 0)
    lane = lax.broadcasted_iota(jnp.int32, (nblk, nblk), 1)
    mine = jnp.broadcast_to(dest_ref[pl.ds(surf, 1), :], (nblk, nblk))
    owner = jnp.sum(jnp.where(line == lane, mine, 0), axis=1, keepdims=True)

    def count(s, total):
        other = jnp.broadcast_to(dest_ref[pl.ds(s, 1), :], (nblk, nblk))
        before = s * nblk + lane < surf * nblk + line
        return total + jnp.where(jnp.logical_and(other == owner, before), 1, 0)

    ranks = lax.fori_loop(0, nsurf, count, jnp.zeros((nblk, nblk), jnp.int32))
    rank = jnp.sum(ranks, axis=1, keepdims=True)
    key_ref[...] = jnp.broadcast_to(owner * nblk + rank, (nblk, LANES))

    bw = bw_ref[...]
    columns = [jnp.broadcast_to(bw[:, o:o + 1], (8, sub)) for o in range(outc)]
    for p in range(PIECES):
        total = chip_b[p]
        for k in range(1, chips):
            copy_b(k, p).wait_recv()
            total = total + recv_b[k - 1, p]
        wall_ref[p] = total * lax.rsqrt(1.0 + total * total)
        for q in range(subs):
            acc = jnp.zeros((8, sub), F32)
            for o in range(outc):
                if o < 8:
                    w = wall_ref[p, o:o + 1, q * sub:(q + 1) * sub]
                else:
                    r = q * extra + o - 8
                    w = wall_ref[p, r:r + 1, piece:piece + sub]
                acc = acc + columns[o] * jnp.broadcast_to(w, (8, sub))
            for i in range(sub // LANES):
                at = (core * PIECES + p) * groups + q * (sub // LANES) + i
                s_ref[pl.ds(pl.multiple_of(at * 8, 8), 8), :] = acc[:, i * LANES:(i + 1) * LANES]
        copy_s(p).start()

    def split(start, rows):
        s = s_ref[pl.ds(start, rows), :]
        hi = s.astype(BF)
        cat_ref[pl.ds(start, rows), :] = jnp.concatenate(
            [hi, (s - hi.astype(F32)).astype(BF)], axis=1)

    for p in range(PIECES):
        split(pl.multiple_of((core * PIECES + p) * groups * 8, groups * 8), groups * 8)

    def wait_c(k, carry):
        copy_c(k).wait()
        return carry

    lax.fori_loop(1, nsurf, wait_c, 0)
    for p in range(PIECES):
        wait_s(p).wait_recv()
        split(pl.multiple_of(((1 - core) * PIECES + p) * groups * 8, groups * 8), groups * 8)

    tiles = cf_ref.shape[0]
    cols = tiles * LANES
    within = lax.broadcasted_iota(jnp.int32, (LANES, LANES), 0)
    chunk = 32

    def pick(k):
        who = lax.rem(surf + k, nsurf)
        cf = cf_all[lax.rem(nsurf - k, nsurf)]
        place = who * nblk + cf // LANES
        spot = cf % LANES
        onehot = jnp.concatenate(
            [jnp.where(within == spot[j:j + 1, :], 1.0, 0.0).astype(BF) for j in range(tiles)], axis=1)
        onehot = jnp.concatenate([onehot, onehot], axis=0)
        want = jnp.concatenate(
            [jnp.broadcast_to(place[j:j + 1, :], (8, LANES)) for j in range(tiles)], axis=1)

        def some(i, acc):
            start = pl.multiple_of(i * chunk * 8, chunk * 8)
            d = jnp.dot(cat_ref[pl.ds(start, chunk * 8), :], onehot, preferred_element_type=F32)
            for b in range(chunk):
                kb = jnp.broadcast_to(key_ref[pl.ds(i * chunk + b, 1), :], (8, LANES))
                kb = jnp.concatenate([kb] * tiles, axis=1)
                acc = acc + jnp.where(want == kb, d[b * 8:(b + 1) * 8], 0.0)
            return acc

        return lax.fori_loop(0, nblk // chunk, some, jnp.zeros((8, cols), F32))

    def give(k, carry):
        gbuf[k] = pick(k)
        copy_g(k).start()
        return carry

    lax.fori_loop(1, nsurf, give, 0)
    own = pick(0)

    def take(k, total):
        copy_g(k).wait()
        return total + rbuf[k]

    src_ref[...] = lax.fori_loop(1, nsurf, take, own)
    for p in range(PIECES):
        copy_a(p).wait_send()
        copy_s(p).wait_send()
        for k in range(1, chips):
            copy_b(k, p).wait_send()


def wall_source(profile, wall_weight, block_dest, col_face, bound_weight):
    nsurf = lax.axis_size("surf")
    chips = lax.axis_size("normal") // 2
    rows, nvars, faces = profile.shape
    outc = wall_weight.shape[0]
    comp = bound_weight.shape[0]
    w = wall_weight.reshape(outc, rows * nvars)
    extra = outc - 8
    w = jnp.concatenate([w[:8]] + [w[8:]] * (8 // extra), axis=0)
    nblk = faces // LANES
    cols = col_face.shape[0]
    length = faces // 2 // PIECES
    packed = length + length // (8 // extra)
    vmem = lambda: pl.BlockSpec(memory_space=pltpu.VMEM)
    dma = pltpu.SemaphoreType.DMA
    piece = (PIECES, 8, packed)
    return pl.pallas_call(
        functools.partial(source_kernel, nsurf, chips, outc),
        out_shape=jax.ShapeDtypeStruct((comp, cols), F32),
        in_specs=[vmem() for _ in range(5)],
        out_specs=vmem(),
        scratch_shapes=[
            pltpu.VMEM(piece, F32), pltpu.VMEM(piece, F32), pltpu.VMEM(piece, F32), pltpu.VMEM(piece, F32),
            pltpu.VMEM((chips - 1,) + piece, F32), pltpu.VMEM(piece, F32),
            pltpu.VMEM((nblk * 8, LANES), F32), pltpu.VMEM((nblk * 8, 2 * LANES), BF),
            pltpu.VMEM((nblk, LANES), jnp.int32), pltpu.VMEM((nsurf, cols // LANES, LANES), jnp.int32),
            pltpu.VMEM((nsurf, comp, cols), F32), pltpu.VMEM((nsurf, comp, cols), F32),
            dma((PIECES,)), dma((PIECES,)), dma((chips - 1, PIECES)), dma((chips - 1, PIECES)),
            dma((PIECES,)), dma((PIECES,)), dma((nsurf,)), dma((nsurf,)), dma((nsurf,)), dma((nsurf,)),
        ],
        compiler_params=pltpu.CompilerParams(
            collective_id=0, has_side_effects=True, vmem_limit_bytes=56 * 2**20),
        name="wall_source",
    )(profile, w, block_dest.reshape(nsurf, nblk), col_face.reshape(cols // LANES, LANES), bound_weight)


def char_kernel(sub, react_ref, inv_ref, src_ref, st_ref, out_ref, mix_ref, pair_ref, t_ref, dr_ref):
    comp, depth, width = st_ref.shape
    grp = 256 // comp

    @pl.when(pl.program_id(0) == 0)
    def _():
        half = 0.5 * react_ref[...]
        hi = half.astype(BF)
        lo = (half - hi.astype(F32)).astype(BF)
        down = lax.broadcasted_iota(jnp.int32, (256, comp), 0) // grp == lax.broadcasted_iota(jnp.int32, (256, comp), 1)
        over = lax.broadcasted_iota(jnp.int32, (comp, 256), 1) // grp == lax.broadcasted_iota(jnp.int32, (comp, 256), 0)
        down = jnp.where(down, 1.0, 0.0).astype(BF)
        over = jnp.where(over, 1.0, 0.0).astype(BF)
        r = lax.broadcasted_iota(jnp.int32, (256, 256), 0)
        c = lax.broadcasted_iota(jnp.int32, (256, 256), 1)
        same = r % grp == c % grp
        for i, part in enumerate((hi, lo)):
            rows = jnp.dot(down, part, preferred_element_type=F32).astype(BF)
            full = jnp.dot(rows, over, preferred_element_type=F32)
            mix_ref[:, i * 256:(i + 1) * 256] = jnp.where(same, full, 0.0).astype(BF)
        pair_ref[...] = jnp.zeros_like(pair_ref)
        pair_ref[:depth, :depth] = inv_ref[...]
        pair_ref[depth:, depth:] = inv_ref[...]

    lead = inv_ref[:, 0:1].astype(F32)
    for c in range(comp):
        t_ref[c] = jnp.tanh(st_ref[c]).astype(BF)
        out_ref[c] = st_ref[c]

    def step(i, carry):
        for h in range(width // sub):
            ls = slice(h * sub, (h + 1) * sub)
            for g in range(depth // grp):
                ds = slice(g * grp, (g + 1) * grp)
                t = t_ref[:, ds, ls].reshape(comp * grp, sub)
                m = jnp.dot(mix_ref[...], jnp.concatenate([t, t], axis=0), preferred_element_type=F32)
                dr_ref[:, ds, ls] = (out_ref[:, ds, ls] + m.reshape(comp, grp, sub)).astype(BF)
        for h in range(width // sub):
            ls = slice(h * sub, (h + 1) * sub)
            for p in range(comp // 2):
                x = dr_ref[2 * p:2 * p + 2, :, ls].reshape(2 * depth, sub)
                n2 = jnp.dot(pair_ref[...], x, preferred_element_type=F32)
                for k in range(2):
                    c = 2 * p + k
                    n = n2[k * depth:(k + 1) * depth] + lead * src_ref[c:c + 1, ls]
                    out_ref[c, :, ls] = n
                    t_ref[c, :, ls] = jnp.tanh(n).astype(BF)
        return carry

    lax.fori_loop(0, STEPS, step, 0)


def char_steps(char_state, source, char_inverse, react, tile=512, sub=256):
    comp, depth, cols = char_state.shape
    full = lambda a: pl.BlockSpec(a.shape, lambda i: (0,) * a.ndim)
    block = pl.BlockSpec((comp, depth, tile), lambda i: (0, 0, i))
    return pl.pallas_call(
        functools.partial(char_kernel, sub),
        grid=(cols // tile,),
        in_specs=[full(react), full(char_inverse), pl.BlockSpec((comp, tile), lambda i: (0, i)), block],
        out_specs=block,
        out_shape=jax.ShapeDtypeStruct(char_state.shape, F32),
        scratch_shapes=[
            pltpu.VMEM((256, 512), BF), pltpu.VMEM((2 * depth, 2 * depth), BF),
            pltpu.VMEM((comp, depth, tile), BF), pltpu.VMEM((comp, depth, tile), BF),
        ],
        compiler_params=pltpu.CompilerParams(vmem_limit_bytes=56 * 2**20),
        name="char_steps",
    )(react, char_inverse, source, char_state)


def body(profile, wall_weight, block_dest, col_face, char_state, char_inverse, react, bound_weight):
    source = wall_source(profile, wall_weight, block_dest, col_face, bound_weight)
    return char_steps(char_state, source, char_inverse, react)


def solution(mesh):
    placed = (
        P("normal", None, "surf"),
        P(None, "normal", None),
        P(),
        P(("surf", "normal")),
        P(None, None, ("surf", "normal")),
        P(),
        P(),
        P(),
    )
    return jax.shard_map(
        body,
        mesh=mesh,
        in_specs=placed,
        out_specs=P(None, None, ("surf", "normal")),
        check_vma=False,
    )
```

profile of v0, /device:TPU:0, one launch (start us, length us, event | category | flops | bytes accessed | tf_op | source)
XLA Modules:
  0.0 55.1 jit_solution(8533902003248130857)
XLA Ops:
  0.0 0.7 %slice.14 = bf16[2,4,16]{2,1,0:T(4,128)(2,1)S(1)} slice(bf16[10,4,16]{2,1,0:T(4,128)(2,1)} %param.9), slice={[8:10], [0:4], [0:16]} | slice | bytes 512 | tf_op jit(solution)/shard_map/slice | solution.py:240
  0.7 0.1 slice.15
  0.8 0.7 %slice.12 = bf16[8,4,16]{2,1,0:T(4,128)(2,1)S(1)} slice(bf16[10,4,16]{2,1,0:T(4,128)(2,1)} %param.9), slice={[0:8], [0:4], [0:16]} | slice | bytes 2048 | tf_op jit(solution)/shard_map/slice | solution.py:240
  1.5 0.1 slice.13
  1.6 1.2 %concatenate.3.w_ref = bf16[16,64]{1,0:T(8,128)(2,1)} concatenate(bf16[8,64]{1,0:T(8,128)(2,1)S(1)} %slice.13, bf16[2,64]{1,0:T(2,128)(2,1)S(1)} %slice.15, bf16[2,64]{1,0:T(2,128)(2,1)S(1)} %slice.15, bf16[2,64]{1,0:T(2,128)(2,1)S(1)} %slice.15, bf16[2,64]{1,0:T(2,128)(2,1)S(1)} %slice.15), dimensions={0} | concatenate | bytes 4096 | tf_op jit(solution)/shard_map/concatenate | solution.py:240
  2.8 32.2 %wall_source.1.src_ref = f32[8,1024]{1,0:T(8,128)} custom-call(bf16[4,16,16384]{2,1,0:T(8,128)(2,1)} %x_ref.1, bf16[16,64]{1,0:T(8,128)(2,1)} %concatenate.3.w_ref, s32[8,128]{1,0:T(8,128)} %bitcast.2, s32[8,128]{1,0:T(8,128)} %bitcast.3, f32[8,10]{1,0:T(8,128)} %bw_ref.1), custom_call_target="tpu_custom_call" | custom-call | tf_op jit(solution)/shard_map/wall_source/pallas_call | solution.py:248
  34.9 20.2 %char_steps.1 = f32[8,128,1024]{2,1,0:T(8,128)} custom-call(f32[8,8]{1,0:T(8,128)} %react_ref.1, bf16[128,128]{1,0:T(8,128)(2,1)} %inv_ref.1, f32[8,1024]{1,0:T(8,128)} %wall_source.1.src_ref, f32[8,128,1024]{2,1,0:T(8,128)} %st_ref.1), custom_call_target="tpu_custom_call" | custom-call | tf_op jit(solution)/shard_map/char_steps/pallas_call | solution.py:324
where the time goes:
time: 55.3 us; the launch traced here: 55.1 us
  Pallas kernels  52.4 us (95%)
  local copies, waits for them, and re-layouts  2.75 us (5%)
    pallas_call x1, Pallas kernels, wall_source(): pl.pallas_call(functools.partial(source_kernel, nsurf, chips, outc), out_...  32.2 us
    pallas_call x1, Pallas kernels, char_steps(): pl.pallas_call(functools.partial(char_kernel, sub), grid=(cols // tile,),...  20.2 us
    slice x4, local copies, waits for them, and re-layouts, wall_source(): w = jnp.concatenate([w[:8]] + [w[8:]] * (8 // extra), axis=0)  1.56 us
    concatenate x1, local copies, waits for them, and re-layouts, wall_source(): w = jnp.concatenate([w[:8]] + [w[8:]] * (8 // extra), axis=0)  1.19 us

commit v1 on v0

--- a/solution.py
+++ b/solution.py
@@ -54,11 +54,14 @@
     lax.fori_loop(1, nsurf, greet, 0)
 
     wide = w_ref[...].astype(F32)
-    row = lax.broadcasted_iota(jnp.int32, wide.shape, 0)
+    row = lax.broadcasted_iota(jnp.int32, (8, depth), 0)
 
     def weights(q):
-        keep = jnp.logical_or(row < 8, (row - 8) // extra == q)
-        return jnp.where(keep, wide, 0.0).astype(BF)
+        below = jnp.zeros((8, depth), F32)
+        for e in range(extra):
+            line = jnp.broadcast_to(wide[8 + e:9 + e], (8, depth))
+            below = jnp.where(row == q * extra + e, line, below)
+        return jnp.concatenate([wide[:8], below], axis=0).astype(BF)
 
     placed = [weights(q) for q in range(subs)]
 
@@ -209,7 +212,8 @@
 
         return lax.fori_loop(0, nblk // chunk, some, jnp.zeros((8, cols), F32))
 
-    def give(k, carry):
+    def give(i, carry):
+        k = nsurf // 2 + (1 - 2 * lax.rem(i + 1, 2)) * (i // 2)
         gbuf[k] = pick(k)
         copy_g(k).start()
         return carry
@@ -237,7 +241,6 @@
     comp = bound_weight.shape[0]
     w = wall_weight.reshape(outc, rows * nvars)
     extra = outc - 8
-    w = jnp.concatenate([w[:8]] + [w[8:]] * (8 // extra), axis=0)
     nblk = faces // LANES
     cols = col_face.shape[0]
     length = faces // 2 // PIECES
@@ -267,24 +270,25 @@
 
 def char_kernel(sub, react_ref, inv_ref, src_ref, st_ref, out_ref, mix_ref, pair_ref, t_ref, dr_ref):
     comp, depth, width = st_ref.shape
-    grp = 256 // comp
+    grp = 128 // comp
+    size = grp * comp
 
     @pl.when(pl.program_id(0) == 0)
     def _():
         half = 0.5 * react_ref[...]
         hi = half.astype(BF)
         lo = (half - hi.astype(F32)).astype(BF)
-        down = lax.broadcasted_iota(jnp.int32, (256, comp), 0) // grp == lax.broadcasted_iota(jnp.int32, (256, comp), 1)
-        over = lax.broadcasted_iota(jnp.int32, (comp, 256), 1) // grp == lax.broadcasted_iota(jnp.int32, (comp, 256), 0)
+        down = lax.broadcasted_iota(jnp.int32, (size, comp), 0) // grp == lax.broadcasted_iota(jnp.int32, (size, comp), 1)
+        over = lax.broadcasted_iota(jnp.int32, (comp, size), 1) // grp == lax.broadcasted_iota(jnp.int32, (comp, size), 0)
         down = jnp.where(down, 1.0, 0.0).astype(BF)
         over = jnp.where(over, 1.0, 0.0).astype(BF)
-        r = lax.broadcasted_iota(jnp.int32, (256, 256), 0)
-        c = lax.broadcasted_iota(jnp.int32, (256, 256), 1)
+        r = lax.broadcasted_iota(jnp.int32, (size, size), 0)
+        c = lax.broadcasted_iota(jnp.int32, (size, size), 1)
         same = r % grp == c % grp
         for i, part in enumerate((hi, lo)):
             rows = jnp.dot(down, part, preferred_element_type=F32).astype(BF)
             full = jnp.dot(rows, over, preferred_element_type=F32)
-            mix_ref[:, i * 256:(i + 1) * 256] = jnp.where(same, full, 0.0).astype(BF)
+            mix_ref[:, i * size:(i + 1) * size] = jnp.where(same, full, 0.0).astype(BF)
         pair_ref[...] = jnp.zeros_like(pair_ref)
         pair_ref[:depth, :depth] = inv_ref[...]
         pair_ref[depth:, depth:] = inv_ref[...]
@@ -314,7 +318,7 @@
                     t_ref[c, :, ls] = jnp.tanh(n).astype(BF)
         return carry
 
-    lax.fori_loop(0, STEPS, step, 0)
+    lax.fori_loop(0, STEPS, step, 0, unroll=STEPS)
 
 
 def char_steps(char_state, source, char_inverse, react, tile=512, sub=256):
@@ -328,7 +332,7 @@
         out_specs=block,
         out_shape=jax.ShapeDtypeStruct(char_state.shape, F32),
         scratch_shapes=[
-            pltpu.VMEM((256, 512), BF), pltpu.VMEM((2 * depth, 2 * depth), BF),
+            pltpu.VMEM((128, 256), BF), pltpu.VMEM((2 * depth, 2 * depth), BF),
             pltpu.VMEM((comp, depth, tile), BF), pltpu.VMEM((comp, depth, tile), BF),
         ],
         compiler_params=pltpu.CompilerParams(vmem_limit_bytes=56 * 2**20),

time: 55.3 us -> 47.1 us (0.85)
  Pallas kernels: 52.4 us -> 45.6 us
  local copies, waits for them, and re-layouts: 2.75 us -> 1.38 us
    pallas_call x1, Pallas kernels: 20.2 us -> 13.3 us  [char_steps(): pl.pallas_call(functools.partial(char_kernel, sub), grid=(cols // tile,),...]
    slice x4 -> x0, local copies, waits for them, and re-layouts: 1.56 us -> none  [wall_source(): w = jnp.concatenate([w[:8]] + [w[8:]] * (8 // extra), axis=0)]
    reshape x0 -> x1, local copies, waits for them, and re-layouts: none -> 1.38 us  [wall_source(): w = wall_weight.reshape(outc, rows * nvars)]
    concatenate x1 -> x0, local copies, waits for them, and re-layouts: 1.19 us -> none  [wall_source(): w = jnp.concatenate([w[:8]] + [w[8:]] * (8 // extra), axis=0)]
where the time goes in v1:
time: 47.1 us; the launch traced here: 47 us
  Pallas kernels  45.6 us (97%)
  local copies, waits for them, and re-layouts  1.38 us (3%)
    pallas_call x1, Pallas kernels, wall_source(): pl.pallas_call(functools.partial(source_kernel, nsurf, chips, outc), out_...  32.2 us
    pallas_call x1, Pallas kernels, char_steps(): pl.pallas_call(functools.partial(char_kernel, sub), grid=(cols // tile,),...  13.3 us
    reshape x1, local copies, waits for them, and re-layouts, wall_source(): w = wall_weight.reshape(outc, rows * nvars)  1.38 us

profile of v1, /device:TPU:0, one launch (start us, length us, event | category | flops | bytes accessed | tf_op | source)
XLA Modules:
  0.0 47.0 jit_solution(17043674209494539726)
XLA Ops:
  0.0 1.4 %reshape.9.w_ref = bf16[10,64]{1,0:T(8,128)(2,1)} reshape(bf16[10,4,16]{2,1,0:T(4,128)(2,1)} %param.9) | data formatting | bytes 2560 | tf_op jit(solution)/shard_map/reshape | solution.py:242
  1.4 32.2 %wall_source.1.src_ref = f32[8,1024]{1,0:T(8,128)} custom-call(bf16[4,16,16384]{2,1,0:T(8,128)(2,1)} %x_ref.1, bf16[10,64]{1,0:T(8,128)(2,1)} %reshape.9.w_ref, s32[8,128]{1,0:T(8,128)} %bitcast.2, s32[8,128]{1,0:T(8,128)} %bitcast.3, f32[8,10]{1,0:T(8,128)} %bw_ref.1), custom_call_target="tpu_custom_call" | custom-call | tf_op jit(solution)/shard_map/wall_source/pallas_call | solution.py:251
  33.6 13.3 %char_steps.1 = f32[8,128,1024]{2,1,0:T(8,128)} custom-call(f32[8,8]{1,0:T(8,128)} %react_ref.1, bf16[128,128]{1,0:T(8,128)(2,1)} %inv_ref.1, f32[8,1024]{1,0:T(8,128)} %wall_source.1.src_ref, f32[8,128,1024]{2,1,0:T(8,128)} %st_ref.1), custom_call_target="tpu_custom_call" | custom-call | tf_op jit(solution)/shard_map/char_steps/pallas_call | solution.py:328
